TPU v7x, 32 devices: a whole 2x2x4 slice. The times are simulated.
32 devices in a mesh: group: 8 (over y, x, core), blk: 4 (over z).
Axes of the slice: x: 2, y: 2, z: 4, core: 2. Of those that a mesh axis runs over, the one named last changes fastest.
Arguments:
- informal: bfloat16 [4096, 1024], P(('group', 'blk')), may hold values from -6 to 6
- formal: bfloat16 [4096, 1024], P(('group', 'blk')), may hold values from -6 to 6
- labels: int32 [4096], P(('group', 'blk')), may hold values from 0 to 511
- temp: float32 [], replicated, may hold values from 2 to 4
- bias: float32 [], replicated, may hold values from -3 to -1
Outputs:
- loss: float32 [4096], P(('group', 'blk'))
- grad_informal: float32 [4096, 1024], P(('group', 'blk'))
- grad_formal: float32 [4096, 1024], P(('group', 'blk'))
- grad_temp: float32 [], replicated
- grad_bias: float32 [], replicated
All inputs are finite; a program needn't handle non-finite values.
Results may differ from a plain program's by a relative error of at most 0.0025.
Values may be sent and summed in bfloat16 or wider, within the bound.
A program may use at most 64 MiB of HBM per device.

v0:
```python
import math

import jax
import jax.numpy as jnp
from jax import lax
from jax.sharding import PartitionSpec as P


def from_behind(shard, axis, by):
    count = lax.axis_size(axis)
    return lax.ppermute(shard, axis, [(i, (i + by) % count) for i in range(count)])


def block_terms(carry, informal, formal, labels, pair, pair_labels, temp, bias):
    loss_sum, grad_x, grad_y, temp_sum, bias_sum = carry
    width = informal.shape[1]
    root = math.sqrt(width)
    scale = temp / root
    other_formal = pair[0]
    other_informal = pair[1]
    raw = (
        lax.dot_general(
            informal, other_formal, (((1,), (1,)), ((), ())), preferred_element_type=jnp.float32
        )
        / root
    )
    logits = temp * raw + bias
    sign = jnp.where(labels[:, None] == pair_labels[None, :], 1.0, -1.0).astype(jnp.float32)
    loss_sum = loss_sum + jnp.sum(jax.nn.softplus(-sign * logits), axis=1)
    slope = -sign * jax.nn.sigmoid(-sign * logits)
    weights = slope.astype(jnp.bfloat16)
    grad_x = grad_x + scale * jnp.dot(weights, other_formal, preferred_element_type=jnp.float32)
    temp_sum = temp_sum + jnp.sum(slope * raw)
    bias_sum = bias_sum + jnp.sum(slope)
    raw_back = (
        lax.dot_general(
            other_informal, formal, (((1,), (1,)), ((), ())), preferred_element_type=jnp.float32
        )
        / root
    )
    logits_back = temp * raw_back + bias
    sign_back = jnp.where(pair_labels[:, None] == labels[None, :], 1.0, -1.0).astype(jnp.float32)
    weights_back = (-sign_back * jax.nn.sigmoid(-sign_back * logits_back)).astype(jnp.bfloat16)
    grad_y = grad_y + scale * lax.dot_general(
        weights_back, other_informal, (((0,), (0,)), ((), ())), preferred_element_type=jnp.float32
    )
    return (loss_sum, grad_x, grad_y, temp_sum, bias_sum)


def on_device(informal, formal, labels, temp, bias):
    rows, width = informal.shape
    ngroup = lax.axis_size("group")
    nblk = lax.axis_size("blk")
    stacked = jnp.stack([formal, informal])
    zero_grad = jnp.zeros((rows, width), jnp.float32)
    start = (
        jnp.zeros((rows,), jnp.float32),
        zero_grad,
        zero_grad,
        jnp.float32(0.0),
        jnp.float32(0.0),
    )

    def turn(step, state):
        carry, pair, pair_labels = state
        carry = block_terms(carry, informal, formal, labels, pair, pair_labels, temp, bias)
        pair, pair_labels = from_behind((pair, pair_labels), "blk", 1)
        return (carry, pair, pair_labels)

    carry, pair, pair_labels = lax.fori_loop(0, nblk - 1, turn, (start, stacked, labels))
    carry = block_terms(carry, informal, formal, labels, pair, pair_labels, temp, bias)
    loss_sum, grad_x, grad_y, temp_sum, bias_sum = carry
    temp_total, bias_total = lax.psum((temp_sum, bias_sum), ("group", "blk"))
    set_size = rows * nblk
    total = jnp.float32(rows * nblk * ngroup) * jnp.float32(set_size)
    loss = loss_sum / set_size
    return (loss, grad_x, grad_y, temp_total / total, bias_total / total)


def solution(mesh):
    in_specs = (P(("group", "blk"), None), P(("group", "blk"), None), P(("group", "blk")), P(), P())
    out_specs = (
        P(("group", "blk")),
        P(("group", "blk"), None),
        P(("group", "blk"), None),
        P(),
        P(),
    )
    return jax.shard_map(
        on_device, mesh=mesh, in_specs=in_specs, out_specs=out_specs, check_vma=False
    )
```

profile of v0, /device:TPU:0, one launch (start us, length us, event | category | flops | bytes accessed | tf_op | source)
XLA Modules:
  0.0 96.6 jit_solution(1949610561260247819)
XLA Ops:
  1.3 1.1 %pad_maximum_fusion = bf16[2,128,1024]{2,1,0:T(8,128)(2,1)S(1)} fusion(bf16[1,128,1024]{2,1,0:T(8,128)(2,1)} %bitcast.50, bf16[1,128,1024]{2,1,0:T(8,128)(2,1)} %bitcast.49), kind=kLoop, calls=%fused_computation.54 | loop fusion | flops 262144 | bytes 1048576 | tf_op jit(solution)/shard_map/stack | solution.py:54
  2.5 0.6 copy-done.2
  3.1 46.2 %while.26 = (s32[]{:T(128)}, f32[128]{0:T(128)S(1)}, f32[128,1024]{1,0:T(8,128)S(1)}, f32[128,1024]{1,0:T(8,128)S(1)}, f32[]{:T(128)}, /*index=5*/f32[]{:T(128)}...) while((s32[]{:T(128)}, f32[128]{0:T(128)S(1)}, ...), condition=%wide.region_4.5_spmd.clone, body=%wide.region_0.4_spmd.clone.sunk | while | flops 135708800 | bytes 6958353 | solution.py:70
  3.2 3.1 %collective-permute-start = (bf16[2,128,1024]{2,1,0:T(8,128)(2,1)S(1)}, bf16[2,128,1024]{2,1,0:T(8,128)(2,1)S(1)}, u32[]{:S(2)}, u32[]{:S(2)}) collective-permute-start(bf16[2,128,1024]{2,1,0:T(8,128)(2,1)S(1)} %copy.30), channel_id=1, source_target_pairs={{0,1},{1,2},{2,3},{3,0},{4,5},{5,6},{6,7},{7,4},{8,9},{9,10},{10,1... | collective-permute-start | bytes 1572872 | tf_op jit(solution)/shard_map/while/body/eval_jaxpr/ppermute | solution.py:11
  6.3 1.6 %collective-permute-start.1 = (s32[128]{0:T(128)S(1)}, s32[128]{0:T(128)S(1)}, u32[]{:S(2)}, u32[]{:S(2)}) collective-permute-start(s32[128]{0:T(128)S(1)} %copy.31), channel_id=1, source_target_pairs={{0,1},{1,2},{2,3},{3,0},{4,5},{5,6},{6,7},{7,4},{8,9},{9,10},{10,1... | collective-permute-start | bytes 1544 | tf_op jit(solution)/shard_map/while/body/eval_jaxpr/ppermute | solution.py:11
  7.8 1.5 %fusion.83 = (f32[]{:T(128)}, f32[]{:T(128)}, f32[128]{0:T(128)S(1)}, f32[128,128]{0,1:T(8,128)S(1)}) fusion(f32[]{:T(128)} %get-tuple-element.412, f32[]{:T(128)} %get-tuple-element.411, s32[128]{0:T(128)S(1)} %copy.31, s32[128]{0:T(128)S(1)} %get-tuple-element.409, bf16[128,1024]{1,0:T(8,128)(2,1)S(1)} %get-tuple-element.410, ...), kind=kOutput, calls=%fused_computation.40.clone.1 | convolution fusion | flops 33898368 | bytes 591376 | tf_op jit(solution)/shard_map/while/body/eval_jaxpr/dot_general | solution.py:22
  9.4 1.0 %fusion.85 = f32[128,1024]{1,0:T(8,128)S(1)} fusion(f32[128,1024]{1,0:T(8,128)S(1)} %get-tuple-element.388, f32[]{:T(128)} %get-tuple-element.411, pred[]{:T(512)S(6)} %compare.3, bf16[2,128,1024]{2,1,0:T(8,128)(2,1)S(1)} %copy.30, f32[128,128]{0,1:T(8,128)S(1)} %get-tuple-element.368, f32[]{:T(128)} %get-tuple-element.412, ...), kind=kOutput, calls=%fused_computation.2.clone.1 | convolution fusion | flops 34127872 | bytes 1378817 | tf_op jit(solution)/shard_map/while/body/eval_jaxpr/dot_general | solution.py:32
  10.4 1.3 %fusion.86 = f32[128,1024]{1,0:T(8,128)S(1)} fusion(bf16[128,1024]{1,0:T(8,128)(2,1)S(1)} %get-tuple-element.413, f32[128,1024]{1,0:T(8,128)S(1)} %get-tuple-element.389, bf16[2,128,1024]{2,1,0:T(8,128)(2,1)S(1)} %copy.30, f32[]{:T(128)} %get-tuple-element.411, pred[]{:T(512)S(6)} %compare.3, s32[128]{0:T(128)S(1)} %copy.31, f32[]{:T(128)} %get-tuple-element.412, ...), kind=kOutput, calls=%fused_computation.3.clone.1 | convolution fusion | flops 67682304 | bytes 1837569 | tf_op jit(solution)/shard_map/while/body/eval_jaxpr/dot_general | solution.py:44
  13.0 7.3 %collective-permute-done.1 = s32[128]{0:T(128)S(1)} collective-permute-done((s32[128]{0:T(128)S(1)}, s32[128]{0:T(128)S(1)}, u32[]{:S(2)}, u32[]{:S(2)}) %collective-permute-start.1) | collective-permute-done | bytes 544 | tf_op jit(solution)/shard_map/while/body/eval_jaxpr/ppermute | solution.py:11
  20.3 0.1 collective-permute-start
  20.4 1.3 %collective-permute-start.1 = (s32[128]{0:T(128)S(1)}, s32[128]{0:T(128)S(1)}, u32[]{:S(2)}, u32[]{:S(2)}) collective-permute-start(s32[128]{0:T(128)S(1)} %copy.31), channel_id=1, source_target_pairs={{0,1},{1,2},{2,3},{3,0},{4,5},{5,6},{6,7},{7,4},{8,9},{9,10},{10,1... | collective-permute-start | bytes 1544 | tf_op jit(solution)/shard_map/while/body/eval_jaxpr/ppermute | solution.py:11
  21.7 1.5 %fusion.83 = (f32[]{:T(128)}, f32[]{:T(128)}, f32[128]{0:T(128)S(1)}, f32[128,128]{0,1:T(8,128)S(1)}) fusion(f32[]{:T(128)} %get-tuple-element.412, f32[]{:T(128)} %get-tuple-element.411, s32[128]{0:T(128)S(1)} %copy.31, s32[128]{0:T(128)S(1)} %get-tuple-element.409, bf16[128,1024]{1,0:T(8,128)(2,1)S(1)} %get-tuple-element.410, ...), kind=kOutput, calls=%fused_computation.40.clone.1 | convolution fusion | flops 33898368 | bytes 591376 | tf_op jit(solution)/shard_map/while/body/eval_jaxpr/dot_general | solution.py:22
  23.2 1.0 %fusion.85 = f32[128,1024]{1,0:T(8,128)S(1)} fusion(f32[128,1024]{1,0:T(8,128)S(1)} %get-tuple-element.388, f32[]{:T(128)} %get-tuple-element.411, pred[]{:T(512)S(6)} %compare.3, bf16[2,128,1024]{2,1,0:T(8,128)(2,1)S(1)} %copy.30, f32[128,128]{0,1:T(8,128)S(1)} %get-tuple-element.368, f32[]{:T(128)} %get-tuple-element.412, ...), kind=kOutput, calls=%fused_computation.2.clone.1 | convolution fusion | flops 34127872 | bytes 1378817 | tf_op jit(solution)/shard_map/while/body/eval_jaxpr/dot_general | solution.py:32
  24.2 1.3 %fusion.86 = f32[128,1024]{1,0:T(8,128)S(1)} fusion(bf16[128,1024]{1,0:T(8,128)(2,1)S(1)} %get-tuple-element.413, f32[128,1024]{1,0:T(8,128)S(1)} %get-tuple-element.389, bf16[2,128,1024]{2,1,0:T(8,128)(2,1)S(1)} %copy.30, f32[]{:T(128)} %get-tuple-element.411, pred[]{:T(512)S(6)} %compare.3, s32[128]{0:T(128)S(1)} %copy.31, f32[]{:T(128)} %get-tuple-element.412, ...), kind=kOutput, calls=%fused_computation.3.clone.1 | convolution fusion | flops 67682304 | bytes 1837569 | tf_op jit(solution)/shard_map/while/body/eval_jaxpr/dot_general | solution.py:44
  26.8 8.5 %collective-permute-done.1 = s32[128]{0:T(128)S(1)} collective-permute-done((s32[128]{0:T(128)S(1)}, s32[128]{0:T(128)S(1)}, u32[]{:S(2)}, u32[]{:S(2)}) %collective-permute-start.1) | collective-permute-done | bytes 544 | tf_op jit(solution)/shard_map/while/body/eval_jaxpr/ppermute | solution.py:11
  35.3 0.1 collective-permute-start
  35.4 0.1 collective-permute-start.1
  35.5 1.5 %fusion.83 = (f32[]{:T(128)}, f32[]{:T(128)}, f32[128]{0:T(128)S(1)}, f32[128,128]{0,1:T(8,128)S(1)}) fusion(f32[]{:T(128)} %get-tuple-element.412, f32[]{:T(128)} %get-tuple-element.411, s32[128]{0:T(128)S(1)} %copy.31, s32[128]{0:T(128)S(1)} %get-tuple-element.409, bf16[128,1024]{1,0:T(8,128)(2,1)S(1)} %get-tuple-element.410, ...), kind=kOutput, calls=%fused_computation.40.clone.1 | convolution fusion | flops 33898368 | bytes 591376 | tf_op jit(solution)/shard_map/while/body/eval_jaxpr/dot_general | solution.py:22
  37.0 1.0 %fusion.85 = f32[128,1024]{1,0:T(8,128)S(1)} fusion(f32[128,1024]{1,0:T(8,128)S(1)} %get-tuple-element.388, f32[]{:T(128)} %get-tuple-element.411, pred[]{:T(512)S(6)} %compare.3, bf16[2,128,1024]{2,1,0:T(8,128)(2,1)S(1)} %copy.30, f32[128,128]{0,1:T(8,128)S(1)} %get-tuple-element.368, f32[]{:T(128)} %get-tuple-element.412, ...), kind=kOutput, calls=%fused_computation.2.clone.1 | convolution fusion | flops 34127872 | bytes 1378817 | tf_op jit(solution)/shard_map/while/body/eval_jaxpr/dot_general | solution.py:32
  38.0 1.3 %fusion.86 = f32[128,1024]{1,0:T(8,128)S(1)} fusion(bf16[128,1024]{1,0:T(8,128)(2,1)S(1)} %get-tuple-element.413, f32[128,1024]{1,0:T(8,128)S(1)} %get-tuple-element.389, bf16[2,128,1024]{2,1,0:T(8,128)(2,1)S(1)} %copy.30, f32[]{:T(128)} %get-tuple-element.411, pred[]{:T(512)S(6)} %compare.3, s32[128]{0:T(128)S(1)} %copy.31, f32[]{:T(128)} %get-tuple-element.412, ...), kind=kOutput, calls=%fused_computation.3.clone.1 | convolution fusion | flops 67682304 | bytes 1837569 | tf_op jit(solution)/shard_map/while/body/eval_jaxpr/dot_general | solution.py:44
  40.6 8.7 %collective-permute-done.1 = s32[128]{0:T(128)S(1)} collective-permute-done((s32[128]{0:T(128)S(1)}, s32[128]{0:T(128)S(1)}, u32[]{:S(2)}, u32[]{:S(2)}) %collective-permute-start.1) | collective-permute-done | bytes 544 | tf_op jit(solution)/shard_map/while/body/eval_jaxpr/ppermute | solution.py:11
  49.3 0.2 fusion.47
  49.5 0.1 copy.11
  50.3 0.2 negate_exponential_fusion
  50.5 0.1 copy.12
  50.6 0.1 copy.13
  50.7 0.6 fusion.61
  52.6 37.4 %all-reduce = (f32[]{:T(128)}, f32[]{:T(128)}) all-reduce(f32[]{:T(128)S(6)} %add.125, f32[]{:T(128)S(6)} %add.126), channel_id=1, replica_groups=mesh['group'=8,'blk'=4] {'group','blk'}, use_global_device_ids=true, to_apply=%region_7.8 | all-reduce | flops 2 | bytes 16 | tf_op jit(solution)/shard_map/psum | solution.py:73
  91.3 0.1 copy.15
  91.4 1.3 %fusion.35 = f32[128,1024]{1,0:T(8,128)} fusion(f32[128,1024]{1,0:T(8,128)S(1)} %get-tuple-element.197, bf16[128,1024]{1,0:T(8,128)(2,1)S(1)} %get-tuple-element.418, bf16[2,128,1024]{2,1,0:T(8,128)(2,1)S(1)} %get-tuple-element.195, f32[]{:T(128)} %mul.105, f32[128,128]{0,1:T(8,128)S(1)} %copy.15, f32[]{:T(128)S(6)} %copy.42), kind=kOutput, calls=%fused_computation.44 | convolution fusion | flops 67518464 | bytes 1901572 | tf_op jit(solution)/shard_map/dot_general | solution.py:44
  92.7 1.0 %fusion.34 = f32[128,1024]{1,0:T(8,128)} fusion(f32[128,1024]{1,0:T(8,128)S(1)} %get-tuple-element.196, f32[]{:T(128)} %mul.105, bf16[2,128,1024]{2,1,0:T(8,128)(2,1)S(1)} %get-tuple-element.195, bf16[128,128]{0,1:T(8,128)(2,1)S(1)} %get-tuple-element.275), kind=kOutput, calls=%fused_computation.43 | convolution fusion | flops 33816576 | bytes 1343492 | tf_op jit(solution)/shard_map/dot_general | solution.py:32
  93.8 0.5 add_multiply_fusion.1
  (21 shorter events, 0.2 us)
Async XLA Ops:
  1.3 1.8 %copy-start = (bf16[128,1024]{1,0:T(8,128)(2,1)S(1)}, bf16[128,1024]{1,0:T(8,128)(2,1)}, u32[]{:S(2)}) copy-start(bf16[128,1024]{1,0:T(8,128)(2,1)} %param.8) | copy-start | bytes 786436
  1.3 1.8 %copy-start.1 = (bf16[128,1024]{1,0:T(8,128)(2,1)S(1)}, bf16[128,1024]{1,0:T(8,128)(2,1)}, u32[]{:S(2)}) copy-start(bf16[128,1024]{1,0:T(8,128)(2,1)} %param.7) | copy-start | bytes 786436
  2.5 0.7 copy-start.2
  3.2 17.1 %collective-permute-start = (bf16[2,128,1024]{2,1,0:T(8,128)(2,1)S(1)}, bf16[2,128,1024]{2,1,0:T(8,128)(2,1)S(1)}, u32[]{:S(2)}, u32[]{:S(2)}) collective-permute-start(bf16[2,128,1024]{2,1,0:T(8,128)(2,1)S(1)} %copy.30), channel_id=1, source_target_pairs={{0,1},{1,2},{2,3},{3,0},{4,5},{5,6},{6,7},{7,4},{8,9},{9,10},{10,1... | collective-permute-start | bytes 1572872 | tf_op jit(solution)/shard_map/while/body/eval_jaxpr/ppermute | solution.py:11
  6.3 14.0 %collective-permute-start.1 = (s32[128]{0:T(128)S(1)}, s32[128]{0:T(128)S(1)}, u32[]{:S(2)}, u32[]{:S(2)}) collective-permute-start(s32[128]{0:T(128)S(1)} %copy.31), channel_id=1, source_target_pairs={{0,1},{1,2},{2,3},{3,0},{4,5},{5,6},{6,7},{7,4},{8,9},{9,10},{10,1... | collective-permute-start | bytes 1544 | tf_op jit(solution)/shard_map/while/body/eval_jaxpr/ppermute | solution.py:11
  20.3 15.0 %collective-permute-start = (bf16[2,128,1024]{2,1,0:T(8,128)(2,1)S(1)}, bf16[2,128,1024]{2,1,0:T(8,128)(2,1)S(1)}, u32[]{:S(2)}, u32[]{:S(2)}) collective-permute-start(bf16[2,128,1024]{2,1,0:T(8,128)(2,1)S(1)} %copy.30), channel_id=1, source_target_pairs={{0,1},{1,2},{2,3},{3,0},{4,5},{5,6},{6,7},{7,4},{8,9},{9,10},{10,1... | collective-permute-start | bytes 1572872 | tf_op jit(solution)/shard_map/while/body/eval_jaxpr/ppermute | solution.py:11
  20.4 14.9 %collective-permute-start.1 = (s32[128]{0:T(128)S(1)}, s32[128]{0:T(128)S(1)}, u32[]{:S(2)}, u32[]{:S(2)}) collective-permute-start(s32[128]{0:T(128)S(1)} %copy.31), channel_id=1, source_target_pairs={{0,1},{1,2},{2,3},{3,0},{4,5},{5,6},{6,7},{7,4},{8,9},{9,10},{10,1... | collective-permute-start | bytes 1544 | tf_op jit(solution)/shard_map/while/body/eval_jaxpr/ppermute | solution.py:11
  35.3 14.0 %collective-permute-start = (bf16[2,128,1024]{2,1,0:T(8,128)(2,1)S(1)}, bf16[2,128,1024]{2,1,0:T(8,128)(2,1)S(1)}, u32[]{:S(2)}, u32[]{:S(2)}) collective-permute-start(bf16[2,128,1024]{2,1,0:T(8,128)(2,1)S(1)} %copy.30), channel_id=1, source_target_pairs={{0,1},{1,2},{2,3},{3,0},{4,5},{5,6},{6,7},{7,4},{8,9},{9,10},{10,1... | collective-permute-start | bytes 1572872 | tf_op jit(solution)/shard_map/while/body/eval_jaxpr/ppermute | solution.py:11
  35.4 13.9 %collective-permute-start.1 = (s32[128]{0:T(128)S(1)}, s32[128]{0:T(128)S(1)}, u32[]{:S(2)}, u32[]{:S(2)}) collective-permute-start(s32[128]{0:T(128)S(1)} %copy.31), channel_id=1, source_target_pairs={{0,1},{1,2},{2,3},{3,0},{4,5},{5,6},{6,7},{7,4},{8,9},{9,10},{10,1... | collective-permute-start | bytes 1544 | tf_op jit(solution)/shard_map/while/body/eval_jaxpr/ppermute | solution.py:11
where the time goes:
time: 97.9 us; the launch traced here: 96.6 us
  blocking collectives  37.4 us (38%)
  waiting for transfers between devices  24.4 us (25%)
  matrix products  14 us (14%)
  between operations  6.89 us (7%)
  starting transfers between devices  6.1 us (6%)
  loops' own time  4.03 us (4%)
  other arithmetic  2.52 us (3%)
  local copies, waits for them, and re-layouts  1.14 us (1%)
    psum x1, blocking collectives, on_device(): temp_total, bias_total = lax.psum((temp_sum, bias_sum), ('group', 'blk'))  37.4 us
    ppermute x6, waiting for transfers between devices, from_behind(): lax.ppermute(shard, axis, [(i, (i + by) % count) for i in range(count)])  24.4 us
    ppermute x6, starting transfers between devices, from_behind(): lax.ppermute(shard, axis, [(i, (i + by) % count) for i in range(count)])  6.1 us
    dot_general x4, matrix products, block_terms(): lax.dot_general(weights_back, other_informal, (((0,), (0,)), ((), ())), p...  5.14 us
    dot_general x4, matrix products, block_terms(): lax.dot_general(informal, other_formal, (((1,), (1,)), ((), ())), preferr...  4.81 us
    dot_general x4, matrix products, block_terms(): jnp.dot(weights, other_formal, preferred_element_type=jnp.float32)  4.1 us
    another operation x1, loops' own time, on_device(): lax.fori_loop(0, nblk - 1, turn, (start, stacked, labels))  4.03 us
  transfers between devices with their start and end apart: 6, of which 3 were waited for; matrix products, arithmetic and copies ran while one was open for 12% of the time, Pallas kernels for 0%

commit v1 on v0

v1 whole, which is shorter than its diff:
```python
import functools
import math

import jax
import jax.numpy as jnp
from jax import lax
from jax.experimental import pallas as pl
from jax.experimental.pallas import tpu as pltpu
from jax.sharding import PartitionSpec as P

MESH = pl.DeviceIdType.MESH
CHUNKS = 8
GRAINS = 2
LAG = 3


def nt_dot(a, b):
    return lax.dot_general(a, b, (((1,), (1,)), ((), ())), preferred_element_type=jnp.float32)


def tn_dot(a, b):
    return lax.dot_general(a, b, (((0,), (0,)), ((), ())), preferred_element_type=jnp.float32)


def kernel(
    n,
    ng,
    x_ref,
    y_ref,
    lab_ref,
    temp_ref,
    bias_ref,
    loss_ref,
    dx_ref,
    dy_ref,
    gtemp_ref,
    gbias_ref,
    ybuf,
    part,
    contrib,
    labbuf,
    labcol,
    loss_acc,
    temp_acc,
    bias_acc,
    sums,
    set_sums,
    all_sums,
    send_sem,
    recv_sem,
    lab_send,
    lab_recv,
    set_send,
    set_recv,
    all_send,
    all_recv,
):
    rows, width = x_ref.shape
    piece = y_ref.shape[1]
    root = math.sqrt(width)
    z = lax.axis_index("blk")
    g = lax.axis_index("group")
    temp = temp_ref[0]
    bias = bias_ref[0]
    grain = rows // GRAINS
    per_grain = CHUNKS // GRAINS

    place = (z, n - 1 - z)

    def real(d, u):
        return u if d == 0 else n - 1 - u

    def y_copy(d, p, c, own=False):
        u = place[d]
        j = z if own else real(d, u - p)
        return pltpu.make_async_remote_copy(
            src_ref=y_ref.at[c] if own else ybuf.at[j, c],
            dst_ref=ybuf.at[j, c],
            send_sem=send_sem.at[d, p, c],
            recv_sem=recv_sem.at[d, p, c],
            device_id={"blk": real(d, u + 1)},
            device_id_type=MESH,
        )

    def y_landing(d, p, c):
        block = ybuf.at[real(d, place[d] - 1 - p), c]
        return pltpu.make_async_remote_copy(
            src_ref=block,
            dst_ref=block,
            send_sem=send_sem.at[d, p, c],
            recv_sem=recv_sem.at[d, p, c],
            device_id={"blk": real(d, place[d] - 1)},
            device_id_type=MESH,
        )

    def part_copy(d, p, c):
        return pltpu.make_async_remote_copy(
            src_ref=part.at[d, p, c],
            dst_ref=part.at[d, p, c],
            send_sem=send_sem.at[d, p, c],
            recv_sem=recv_sem.at[d, p, c],
            device_id={"blk": real(d, place[d] + 1)},
            device_id_type=MESH,
        )

    def small_copy(src, slots, sends, recvs, axis, me, k, count):
        to = lax.rem(me + k, count)
        return pltpu.make_async_remote_copy(
            src_ref=src,
            dst_ref=slots.at[me],
            send_sem=sends.at[k],
            recv_sem=recvs.at[me],
            device_id={axis: to},
            device_id_type=MESH,
        )

    def small_landing(slots, sends, recvs, axis, me, k, count):
        source = lax.rem(me + k, count)
        return pltpu.make_async_remote_copy(
            src_ref=slots.at[source],
            dst_ref=slots.at[source],
            send_sem=sends.at[k],
            recv_sem=recvs.at[source],
            device_id={axis: source},
            device_id_type=MESH,
        )

    def each(count, what):
        def turn(k, carry):
            what(k)
            return carry

        lax.fori_loop(1, count, turn, 0)

    barrier = pltpu.get_barrier_semaphore()

    def greet(axis, me, count, k):
        pl.semaphore_signal(
            barrier, inc=1, device_id={axis: lax.rem(me + k, count)}, device_id_type=MESH
        )

    each(n, functools.partial(greet, "blk", z, n))
    each(ng, functools.partial(greet, "group", g, ng))
    pl.semaphore_wait(barrier, n + ng - 2)

    each(n, lambda k: small_copy(lab_ref, labbuf, lab_send, lab_recv, "blk", z, k, n).start())
    for c in range(CHUNKS):
        for d in range(2):

            @pl.when(place[d] < n - 1)
            def _():
                y_copy(d, 0, c, own=True).start()

    def column(labels):
        return jnp.transpose(jnp.broadcast_to(labels, (rows, rows)))

    def pieces(k):
        return pl.ds(pl.multiple_of(k * per_grain, per_grain), per_grain)

    def compute(y, j, k):
        at = pl.ds(pl.multiple_of(k * grain, grain), grain)
        y = y.reshape(grain, width)
        x = x_ref[...]
        raw = nt_dot(y, x) / root
        logits = temp * raw + bias
        positive = labcol[j, at] == lab_ref[...]
        turned = jnp.where(positive, -logits, logits)
        small = jnp.exp(-jnp.abs(turned))
        loss = jnp.maximum(turned, 0.0) + jnp.log1p(small)
        sigmoid = jnp.where(turned >= 0, 1.0, small) / (1.0 + small)
        slope = jnp.where(positive, -sigmoid, sigmoid)
        loss_acc[...] += loss
        temp_acc[...] += slope * raw
        bias_acc[...] += slope
        weights = slope.astype(jnp.bfloat16)
        back = jnp.dot(weights, x, preferred_element_type=jnp.float32)
        contrib[j, pieces(k)] = back.reshape(per_grain, piece, width)
        dx_ref[...] += tn_dot(weights, y)

    loss_acc[...] = jnp.zeros_like(loss_acc)
    temp_acc[...] = jnp.zeros_like(temp_acc)
    bias_acc[...] = jnp.zeros_like(bias_acc)
    dx_ref[...] = jnp.zeros_like(dx_ref)
    labcol[z] = column(lab_ref[...])
    for k in range(GRAINS):
        compute(y_ref[pl.ds(k * per_grain, per_grain)], z, k)

    def share_set():
        total = jnp.concatenate(
            [
                jnp.sum(temp_acc[...], axis=0, keepdims=True),
                jnp.sum(bias_acc[...], axis=0, keepdims=True),
                jnp.zeros((6, rows), jnp.float32),
            ],
            axis=0,
        )
        sums[0] = total
        set_sums[z] = total
        each(
            n,
            lambda k: small_copy(
                sums.at[0], set_sums, set_send, set_recv, "blk", z, k, n
            ).start(),
        )

    def share_all():
        each(n, lambda k: small_landing(set_sums, set_send, set_recv, "blk", z, k, n).wait_recv())
        total = set_sums[0]
        for j in range(1, n):
            total = total + set_sums[j]
        sums[1] = total
        all_sums[g] = total
        each(
            ng,
            lambda k: small_copy(
                sums.at[1], all_sums, all_send, all_recv, "group", g, k, ng
            ).start(),
        )

    def arrived(d, p, c):
        u = place[d]

        @pl.when(p < u)
        def _():
            y_landing(d, p, c).wait_recv()

            @pl.when(u < n - 1)
            def _():
                y_copy(d, p + 1, c).start()

        @pl.when(p > u)
        def _():
            part_copy(d, p, c).wait_recv()
            both = contrib[real(d, p), c] + part[d, p, c].astype(jnp.float32)
            part[d, p, c] = both.astype(jnp.bfloat16)
            part_copy(d, p, c).start()

        @pl.when(p == u)
        def _():
            part_copy(d, p, c).wait_recv()
            contrib[z, c] += part[d, p, c].astype(jnp.float32)

    def use(d, p, c):
        u = place[d]

        @pl.when((p < u) & (lax.rem(c + 1, per_grain) == 0))
        def _():
            k = lax.div(c, per_grain)
            j = real(d, u - 1 - p)
            compute(ybuf[j, pieces(k)], j, k)

            @pl.when(u == n - 1)
            def _():
                part[1 - d, p + 1, pieces(k)] = contrib[j, pieces(k)].astype(jnp.bfloat16)
                for i in range(per_grain):
                    part_copy(1 - d, p + 1, k * per_grain + i).start()

    def take(k):
        small_landing(labbuf, lab_send, lab_recv, "blk", z, k, n).wait_recv()
        source = lax.rem(z + k, n)
        labcol[source] = column(labbuf[source])

    each(n, take)

    lags = [jnp.minimum(LAG * jnp.maximum(u - 1, 0), CHUNKS) for u in place]
    last = jnp.maximum(lags[0], lags[1])
    computed = (n - 1) * CHUNKS + last

    def step(t, carry):
        for what in (arrived, use):
            for d in range(2):
                f = t - lags[d]

                @pl.when((place[d] > 0) & (f >= 0) & (f < n * CHUNKS))
                def _():
                    what(d, lax.div(f, CHUNKS), lax.rem(f, CHUNKS))

        @pl.when(t == computed)
        def _():
            share_set()

        @pl.when(t == computed + CHUNKS // 2)
        def _():
            share_all()

        return carry

    lax.fori_loop(0, n * CHUNKS + last, step, 0)

    scale = temp / root
    dx_ref[...] = scale * dx_ref[...]
    dy_ref[...] = scale * contrib[z].reshape(rows, width)
    loss_ref[...] = jnp.sum(loss_acc[...], axis=0, keepdims=True) / (rows * n)

    each(ng, lambda k: small_landing(all_sums, all_send, all_recv, "group", g, k, ng).wait_recv())
    total = all_sums[0]
    for j in range(1, ng):
        total = total + all_sums[j]
    pairs = float(rows * n * ng) * float(rows * n)
    gtemp_ref[0] = jnp.sum(total[0:1]) / pairs
    gbias_ref[0] = jnp.sum(total[1:2]) / pairs

    def sent(f, carry):
        p, c = lax.div(f, CHUNKS), lax.rem(f, CHUNKS)
        for d in range(2):
            u = place[d]

            @pl.when((u < n - 1) & (p <= u))
            def _():
                y_copy(d, p, c).wait_send()

            @pl.when((u < n - 1) & (p > u))
            def _():
                part_copy(d, p, c).wait_send()

        return carry

    lax.fori_loop(0, n * CHUNKS, sent, 0)
    each(n, lambda k: small_copy(lab_ref, labbuf, lab_send, lab_recv, "blk", z, k, n).wait_send())
    each(
        n,
        lambda k: small_copy(sums.at[0], set_sums, set_send, set_recv, "blk", z, k, n).wait_send(),
    )
    each(
        ng,
        lambda k: small_copy(
            sums.at[1], all_sums, all_send, all_recv, "group", g, k, ng
        ).wait_send(),
    )


def on_device(informal, formal, labels, temp, bias):
    rows, width = informal.shape
    ng = lax.axis_size("group")
    n = lax.axis_size("blk")
    vmem = pl.BlockSpec(memory_space=pltpu.VMEM)
    smem = pl.BlockSpec(memory_space=pltpu.SMEM)
    f32 = jnp.float32
    dma = pltpu.SemaphoreType.DMA
    loss, dx, dy, gtemp, gbias = pl.pallas_call(
        functools.partial(kernel, n, ng),
        out_shape=(
            jax.ShapeDtypeStruct((1, rows), f32),
            jax.ShapeDtypeStruct((rows, width), f32),
            jax.ShapeDtypeStruct((rows, width), f32),
            jax.ShapeDtypeStruct((1,), f32),
            jax.ShapeDtypeStruct((1,), f32),
        ),
        in_specs=[vmem, vmem, vmem, smem, smem],
        out_specs=(vmem, vmem, vmem, smem, smem),
        scratch_shapes=[
            pltpu.VMEM((n, CHUNKS, rows // CHUNKS, width), jnp.bfloat16),
            pltpu.VMEM((2, n, CHUNKS, rows // CHUNKS, width), jnp.bfloat16),
            pltpu.VMEM((n, CHUNKS, rows // CHUNKS, width), f32),
            pltpu.VMEM((n, 1, rows), jnp.int32),
            pltpu.VMEM((n, rows, rows), jnp.int32),
            pltpu.VMEM((rows // GRAINS, rows), f32),
            pltpu.VMEM((rows // GRAINS, rows), f32),
            pltpu.VMEM((rows // GRAINS, rows), f32),
            pltpu.VMEM((2, 8, rows), f32),
            pltpu.VMEM((n, 8, rows), f32),
            pltpu.VMEM((ng, 8, rows), f32),
            dma((2, n, CHUNKS)),
            dma((2, n, CHUNKS)),
            dma((n,)),
            dma((n,)),
            dma((n,)),
            dma((n,)),
            dma((ng,)),
            dma((ng,)),
        ],
        compiler_params=pltpu.CompilerParams(
            collective_id=0, has_side_effects=True, vmem_limit_bytes=48 * 2**20
        ),
    )(
        informal,
        formal.reshape(CHUNKS, rows // CHUNKS, width),
        labels.reshape(1, rows),
        temp.reshape(1),
        bias.reshape(1),
    )
    return loss.reshape(rows), dx, dy, gtemp.reshape(()), gbias.reshape(())


def solution(mesh):
    in_specs = (P(("group", "blk"), None), P(("group", "blk"), None), P(("group", "blk")), P(), P())
    out_specs = (
        P(("group", "blk")),
        P(("group", "blk"), None),
        P(("group", "blk"), None),
        P(),
        P(),
    )
    return jax.shard_map(
        on_device, mesh=mesh, in_specs=in_specs, out_specs=out_specs, check_vma=False
    )
```

time: 97.9 us -> 53.2 us (0.54); the launches traced: 96.6 us -> 53 us
  Pallas kernels: 0 us -> 42.9 us
  blocking collectives: 37.4 us -> 0 us
  waiting for transfers between devices: 24.4 us -> 0 us
  matrix products: 14 us -> 0 us
  starting transfers between devices: 6.1 us -> 0 us
  loops' own time: 4.03 us -> 0 us
  local copies, waits for them, and re-layouts: 1.14 us -> 4.65 us
  other arithmetic: 2.52 us -> 0 us
  between operations: 6.89 us -> 5.43 us
    pallas_call x0 -> x1, Pallas kernels: none -> 42.9 us  [on_device(): pl.pallas_call(functools.partial(kernel, n, ng), out_shape=(jax.ShapeDtyp...]
    psum x1 -> x0, blocking collectives: 37.4 us -> none  [on_device(): temp_total, bias_total = lax.psum((temp_sum, bias_sum), ('group', 'blk'))]
    ppermute x6 -> x0, waiting for transfers between devices: 24.4 us -> none  [from_behind(): lax.ppermute(shard, axis, [(i, (i + by) % count) for i in range(count)])]
    dot_general x12 -> x0, matrix products: 14 us -> none  [the longest x4 5.14 us: block_terms(): lax.dot_general(weights_back, other_informal, (((0,), (0,)), ((), ())), p...]
    ppermute x6 -> x0, starting transfers between devices: 6.1 us -> none  [from_behind(): lax.ppermute(shard, axis, [(i, (i + by) % count) for i in range(count)])]
    another operation x1 -> x0, loops' own time: 4.03 us -> none  [on_device(): lax.fori_loop(0, nblk - 1, turn, (start, stacked, labels))]
    unnamed x7 -> x9, local copies, waits for them, and re-layouts: 0.66 us -> 4.65 us
    another operation x1 -> x0, other arithmetic: 1.13 us -> none  [on_device(): stacked = jnp.stack([formal, informal])]
  transfers between devices with their start and end apart: 6 -> 0, of which waited for: 3 -> 0; matrix products, arithmetic and copies ran while one was open for 12% -> 0% of each run, Pallas kernels for 0% -> 0%
where the time goes in v1:
time: 53.2 us; the launch traced here: 53 us
  Pallas kernels  42.9 us (81%)
  between operations  5.43 us (10%)
  local copies, waits for them, and re-layouts  4.65 us (9%)
    pallas_call x1, Pallas kernels, on_device(): pl.pallas_call(functools.partial(kernel, n, ng), out_shape=(jax.ShapeDtyp...  42.9 us
    unnamed x9, local copies, waits for them, and re-layouts  4.65 us

profile of v1, /device:TPU:0, one launch (start us, length us, event | category | flops | bytes accessed | tf_op | source)
XLA Modules:
  0.0 53.0 jit_solution(17741696827257646055)
XLA Ops:
  1.9 0.0 copy-start.2
  1.9 0.6 %copy-done.2 = s32[128]{0:T(128)S(1)} copy-done((s32[128]{0:T(128)S(1)}, s32[128]{0:T(128)}, u32[]{:S(2)}) %copy-start.2) | copy-done | bytes 536
  2.6 0.0 copy-start
  2.6 0.9 %copy-done = bf16[128,1024]{1,0:T(8,128)(2,1)S(1)} copy-done((bf16[128,1024]{1,0:T(8,128)(2,1)S(1)}, bf16[128,1024]{1,0:T(8,128)(2,1)}, u32[]{:S(2)}) %copy-start) | copy-done | bytes 262168
  3.5 0.0 copy-start.1
  3.5 0.9 %copy-done.1 = bf16[128,1024]{1,0:T(8,128)(2,1)S(1)} copy-done((bf16[128,1024]{1,0:T(8,128)(2,1)S(1)}, bf16[128,1024]{1,0:T(8,128)(2,1)}, u32[]{:S(2)}) %copy-start.1) | copy-done | bytes 262168
  4.5 42.9 %shard_map.92 = (f32[1,128]{1,0:T(1,128)S(1)}, f32[128,1024]{1,0:T(8,128)S(1)}, f32[128,1024]{1,0:T(8,128)S(1)}, f32[1]{0:T(128)}, f32[1]{0:T(128)}) custom-call(bf16[128,1024]{1,0:T(8,128)(2,1)S(1)} %copy-done, bf16[8,16,1024]{2,1,0:T(8,128)(2,1)S(1)} %bitcast.9, s32[1,128]{1,0:T(1,128)S(1)} %bitcast.10, f32[1]{0:T(128)} %bitcast.7.temp_ref, f32[1]{0:T(128)} %bitcast.8.bias_ref), custom_call_target="tpu_custom_call" | custom-call | tf_op jit(solution)/shard_map/pallas_call | solution.py:340
  47.4 0.5 copy.17
  47.9 0.8 %copy.18 = f32[128,1024]{1,0:T(8,128)} copy(f32[128,1024]{1,0:T(8,128)S(1)} %get-tuple-element.21) | data formatting | bytes 1048576
  48.7 0.8 %copy.19 = f32[128,1024]{1,0:T(8,128)} copy(f32[128,1024]{1,0:T(8,128)S(1)} %get-tuple-element.22) | data formatting | bytes 1048576
Async XLA Ops:
  1.9 0.7 %copy-start.2 = (s32[128]{0:T(128)S(1)}, s32[128]{0:T(128)}, u32[]{:S(2)}) copy-start(s32[128]{0:T(128)} %param.7) | copy-start | bytes 1540
  2.6 0.9 %copy-start = (bf16[128,1024]{1,0:T(8,128)(2,1)S(1)}, bf16[128,1024]{1,0:T(8,128)(2,1)}, u32[]{:S(2)}) copy-start(bf16[128,1024]{1,0:T(8,128)(2,1)} %x_ref.1) | copy-start | bytes 786436
  3.5 0.9 %copy-start.1 = (bf16[128,1024]{1,0:T(8,128)(2,1)S(1)}, bf16[128,1024]{1,0:T(8,128)(2,1)}, u32[]{:S(2)}) copy-start(bf16[128,1024]{1,0:T(8,128)(2,1)} %param.6) | copy-start | bytes 786436

commit v2 on v1

--- a/solution.py
+++ b/solution.py
@@ -260,13 +260,15 @@
         source = lax.rem(z + k, n)
         labcol[source] = column(labbuf[source])
 
-    each(n, take)
-
     lags = [jnp.minimum(LAG * jnp.maximum(u - 1, 0), CHUNKS) for u in place]
     last = jnp.maximum(lags[0], lags[1])
     computed = (n - 1) * CHUNKS + last
 
     def step(t, carry):
+        @pl.when(t == per_grain - 1)
+        def _():
+            each(n, take)
+
         for what in (arrived, use):
             for d in range(2):
                 f = t - lags[d]

time: 53.2 us -> 53.2 us (level)
  no operation moved by 1% of the time
where the time goes in v2:
time: 53.2 us; the launch traced here: 53 us
  Pallas kernels  42.9 us (81%)
  between operations  5.43 us (10%)
  local copies, waits for them, and re-layouts  4.65 us (9%)
    pallas_call x1, Pallas kernels, on_device(): pl.pallas_call(functools.partial(kernel, n, ng), out_shape=(jax.ShapeDtyp...  42.9 us
    unnamed x9, local copies, waits for them, and re-layouts  4.65 us

profile of v2, /device:TPU:0, one launch (start us, length us, event | category | flops | bytes accessed | tf_op | source)
XLA Modules:
  0.0 53.0 jit_solution(16531468831543944167)
XLA Ops:
  1.9 0.0 copy-start.2
  1.9 0.6 %copy-done.2 = s32[128]{0:T(128)S(1)} copy-done((s32[128]{0:T(128)S(1)}, s32[128]{0:T(128)}, u32[]{:S(2)}) %copy-start.2) | copy-done | bytes 536
  2.6 0.0 copy-start
  2.6 0.9 %copy-done = bf16[128,1024]{1,0:T(8,128)(2,1)S(1)} copy-done((bf16[128,1024]{1,0:T(8,128)(2,1)S(1)}, bf16[128,1024]{1,0:T(8,128)(2,1)}, u32[]{:S(2)}) %copy-start) | copy-done | bytes 262168
  3.5 0.0 copy-start.1
  3.5 0.9 %copy-done.1 = bf16[128,1024]{1,0:T(8,128)(2,1)S(1)} copy-done((bf16[128,1024]{1,0:T(8,128)(2,1)S(1)}, bf16[128,1024]{1,0:T(8,128)(2,1)}, u32[]{:S(2)}) %copy-start.1) | copy-done | bytes 262168
  4.5 42.9 %shard_map.92 = (f32[1,128]{1,0:T(1,128)S(1)}, f32[128,1024]{1,0:T(8,128)S(1)}, f32[128,1024]{1,0:T(8,128)S(1)}, f32[1]{0:T(128)}, f32[1]{0:T(128)}) custom-call(bf16[128,1024]{1,0:T(8,128)(2,1)S(1)} %copy-done, bf16[8,16,1024]{2,1,0:T(8,128)(2,1)S(1)} %bitcast.9, s32[1,128]{1,0:T(1,128)S(1)} %bitcast.10, f32[1]{0:T(128)} %bitcast.7.temp_ref, f32[1]{0:T(128)} %bitcast.8.bias_ref), custom_call_target="tpu_custom_call" | custom-call | tf_op jit(solution)/shard_map/pallas_call | solution.py:342
  47.4 0.5 copy.17
  47.9 0.8 %copy.18 = f32[128,1024]{1,0:T(8,128)} copy(f32[128,1024]{1,0:T(8,128)S(1)} %get-tuple-element.21) | data formatting | bytes 1048576
  48.7 0.8 %copy.19 = f32[128,1024]{1,0:T(8,128)} copy(f32[128,1024]{1,0:T(8,128)S(1)} %get-tuple-element.22) | data formatting | bytes 1048576
Async XLA Ops:
  1.9 0.7 %copy-start.2 = (s32[128]{0:T(128)S(1)}, s32[128]{0:T(128)}, u32[]{:S(2)}) copy-start(s32[128]{0:T(128)} %param.7) | copy-start | bytes 1540
  2.6 0.9 %copy-start = (bf16[128,1024]{1,0:T(8,128)(2,1)S(1)}, bf16[128,1024]{1,0:T(8,128)(2,1)}, u32[]{:S(2)}) copy-start(bf16[128,1024]{1,0:T(8,128)(2,1)} %x_ref.1) | copy-start | bytes 786436
  3.5 0.9 %copy-start.1 = (bf16[128,1024]{1,0:T(8,128)(2,1)S(1)}, bf16[128,1024]{1,0:T(8,128)(2,1)}, u32[]{:S(2)}) copy-start(bf16[128,1024]{1,0:T(8,128)(2,1)} %param.6) | copy-start | bytes 786436

commit v3 on v1

--- a/solution.py
+++ b/solution.py
@@ -132,6 +132,22 @@
 
         lax.fori_loop(1, count, turn, 0)
 
+    rounds = ng.bit_length() - 1
+    assert ng == 1 << rounds
+
+    def mate(r):
+        return g + (1 << r) * (1 - 2 * lax.rem(lax.div(g, 1 << r), 2))
+
+    def pair_copy(r):
+        return pltpu.make_async_remote_copy(
+            src_ref=sums.at[1 + r],
+            dst_ref=all_sums.at[r],
+            send_sem=all_send.at[r],
+            recv_sem=all_recv.at[r],
+            device_id={"group": mate(r)},
+            device_id_type=MESH,
+        )
+
     barrier = pltpu.get_barrier_semaphore()
 
     def greet(axis, me, count, k):
@@ -140,8 +156,9 @@
         )
 
     each(n, functools.partial(greet, "blk", z, n))
-    each(ng, functools.partial(greet, "group", g, ng))
-    pl.semaphore_wait(barrier, n + ng - 2)
+    for r in range(rounds):
+        pl.semaphore_signal(barrier, inc=1, device_id={"group": mate(r)}, device_id_type=MESH)
+    pl.semaphore_wait(barrier, n - 1 + rounds)
 
     each(n, lambda k: small_copy(lab_ref, labbuf, lab_send, lab_recv, "blk", z, k, n).start())
     for c in range(CHUNKS):
@@ -209,13 +226,13 @@
         for j in range(1, n):
             total = total + set_sums[j]
         sums[1] = total
-        all_sums[g] = total
-        each(
-            ng,
-            lambda k: small_copy(
-                sums.at[1], all_sums, all_send, all_recv, "group", g, k, ng
-            ).start(),
-        )
+        pair_copy(0).start()
+
+    def join(r):
+        pair_copy(r - 1).wait_recv()
+        sums[1 + r] = sums[r] + all_sums[r - 1]
+        if r < rounds:
+            pair_copy(r).start()
 
     def arrived(d, p, c):
         u = place[d]
@@ -279,9 +296,14 @@
         def _():
             share_set()
 
-        @pl.when(t == computed + CHUNKS // 2)
-        def _():
-            share_all()
+        for r in range(rounds):
+
+            @pl.when(t == computed + min(2 + 2 * r, CHUNKS - 1))
+            def _():
+                if r == 0:
+                    share_all()
+                else:
+                    join(r)
 
         return carry
 
@@ -292,10 +314,8 @@
     dy_ref[...] = scale * contrib[z].reshape(rows, width)
     loss_ref[...] = jnp.sum(loss_acc[...], axis=0, keepdims=True) / (rows * n)
 
-    each(ng, lambda k: small_landing(all_sums, all_send, all_recv, "group", g, k, ng).wait_recv())
-    total = all_sums[0]
-    for j in range(1, ng):
-        total = total + all_sums[j]
+    join(rounds)
+    total = sums[1 + rounds]
     pairs = float(rows * n * ng) * float(rows * n)
     gtemp_ref[0] = jnp.sum(total[0:1]) / pairs
     gbias_ref[0] = jnp.sum(total[1:2]) / pairs
@@ -321,12 +341,8 @@
         n,
         lambda k: small_copy(sums.at[0], set_sums, set_send, set_recv, "blk", z, k, n).wait_send(),
     )
-    each(
-        ng,
-        lambda k: small_copy(
-            sums.at[1], all_sums, all_send, all_recv, "group", g, k, ng
-        ).wait_send(),
-    )
+    for r in range(rounds):
+        pair_copy(r).wait_send()
 
 
 def on_device(informal, formal, labels, temp, bias):
@@ -357,7 +373,7 @@
             pltpu.VMEM((rows // GRAINS, rows), f32),
             pltpu.VMEM((rows // GRAINS, rows), f32),
             pltpu.VMEM((rows // GRAINS, rows), f32),
-            pltpu.VMEM((2, 8, rows), f32),
+            pltpu.VMEM((ng.bit_length() + 1, 8, rows), f32),
             pltpu.VMEM((n, 8, rows), f32),
             pltpu.VMEM((ng, 8, rows), f32),
             dma((2, n, CHUNKS)),

time: 53.2 us -> 58.5 us (1.100)
  Pallas kernels: 42.9 us -> 48.1 us
    pallas_call x1, Pallas kernels: 42.9 us -> 48.1 us  [on_device(): pl.pallas_call(functools.partial(kernel, n, ng), out_shape=(jax.ShapeDtyp...]
where the time goes in v3:
time: 58.5 us; the launch traced here: 58.2 us
  Pallas kernels  48.1 us (82%)
  between operations  5.43 us (9%)
  local copies, waits for them, and re-layouts  4.65 us (8%)
    pallas_call x1, Pallas kernels, on_device(): pl.pallas_call(functools.partial(kernel, n, ng), out_shape=(jax.ShapeDtyp...  48.1 us
    unnamed x9, local copies, waits for them, and re-layouts  4.65 us

profile of v3, /device:TPU:0, one launch (start us, length us, event | category | flops | bytes accessed | tf_op | source)
XLA Modules:
  0.0 58.2 jit_solution(17057505984353455935)
XLA Ops:
  1.9 0.0 copy-start.2
  1.9 0.6 %copy-done.2 = s32[128]{0:T(128)S(1)} copy-done((s32[128]{0:T(128)S(1)}, s32[128]{0:T(128)}, u32[]{:S(2)}) %copy-start.2) | copy-done | bytes 536
  2.6 0.0 copy-start
  2.6 0.9 %copy-done = bf16[128,1024]{1,0:T(8,128)(2,1)S(1)} copy-done((bf16[128,1024]{1,0:T(8,128)(2,1)S(1)}, bf16[128,1024]{1,0:T(8,128)(2,1)}, u32[]{:S(2)}) %copy-start) | copy-done | bytes 262168
  3.5 0.0 copy-start.1
  3.5 0.9 %copy-done.1 = bf16[128,1024]{1,0:T(8,128)(2,1)S(1)} copy-done((bf16[128,1024]{1,0:T(8,128)(2,1)S(1)}, bf16[128,1024]{1,0:T(8,128)(2,1)}, u32[]{:S(2)}) %copy-start.1) | copy-done | bytes 262168
  4.5 48.1 %shard_map.92 = (f32[1,128]{1,0:T(1,128)S(1)}, f32[128,1024]{1,0:T(8,128)S(1)}, f32[128,1024]{1,0:T(8,128)S(1)}, f32[1]{0:T(128)}, f32[1]{0:T(128)}) custom-call(bf16[128,1024]{1,0:T(8,128)(2,1)S(1)} %copy-done, bf16[8,16,1024]{2,1,0:T(8,128)(2,1)S(1)} %bitcast.9, s32[1,128]{1,0:T(1,128)S(1)} %bitcast.10, f32[1]{0:T(128)} %bitcast.7.temp_ref, f32[1]{0:T(128)} %bitcast.8.bias_ref), custom_call_target="tpu_custom_call" | custom-call | tf_op jit(solution)/shard_map/pallas_call | solution.py:356
  52.6 0.5 copy.17
  53.1 0.8 %copy.18 = f32[128,1024]{1,0:T(8,128)} copy(f32[128,1024]{1,0:T(8,128)S(1)} %get-tuple-element.21) | data formatting | bytes 1048576
  53.9 0.8 %copy.19 = f32[128,1024]{1,0:T(8,128)} copy(f32[128,1024]{1,0:T(8,128)S(1)} %get-tuple-element.22) | data formatting | bytes 1048576
Async XLA Ops:
  1.9 0.7 %copy-start.2 = (s32[128]{0:T(128)S(1)}, s32[128]{0:T(128)}, u32[]{:S(2)}) copy-start(s32[128]{0:T(128)} %param.7) | copy-start | bytes 1540
  2.6 0.9 %copy-start = (bf16[128,1024]{1,0:T(8,128)(2,1)S(1)}, bf16[128,1024]{1,0:T(8,128)(2,1)}, u32[]{:S(2)}) copy-start(bf16[128,1024]{1,0:T(8,128)(2,1)} %x_ref.1) | copy-start | bytes 786436
  3.5 0.9 %copy-start.1 = (bf16[128,1024]{1,0:T(8,128)(2,1)S(1)}, bf16[128,1024]{1,0:T(8,128)(2,1)}, u32[]{:S(2)}) copy-start(bf16[128,1024]{1,0:T(8,128)(2,1)} %param.6) | copy-start | bytes 786436

commit v4 on v1

--- a/solution.py
+++ b/solution.py
@@ -11,7 +11,7 @@
 MESH = pl.DeviceIdType.MESH
 CHUNKS = 8
 GRAINS = 2
-LAG = 3
+LAG = 2
 
 
 def nt_dot(a, b):

time: 53.2 us -> 57.8 us (1.086)
  Pallas kernels: 42.9 us -> 47.5 us
    pallas_call x1, Pallas kernels: 42.9 us -> 47.5 us  [on_device(): pl.pallas_call(functools.partial(kernel, n, ng), out_shape=(jax.ShapeDtyp...]
where the time goes in v4:
time: 57.8 us; the launch traced here: 57.5 us
  Pallas kernels  47.5 us (82%)
  between operations  5.43 us (9%)
  local copies, waits for them, and re-layouts  4.65 us (8%)
    pallas_call x1, Pallas kernels, on_device(): pl.pallas_call(functools.partial(kernel, n, ng), out_shape=(jax.ShapeDtyp...  47.5 us
    unnamed x9, local copies, waits for them, and re-layouts  4.65 us

profile of v4, /device:TPU:0, one launch (start us, length us, event | category | flops | bytes accessed | tf_op | source)
XLA Modules:
  0.0 57.5 jit_solution(2729067484283219708)
XLA Ops:
  1.9 0.0 copy-start.2
  1.9 0.6 %copy-done.2 = s32[128]{0:T(128)S(1)} copy-done((s32[128]{0:T(128)S(1)}, s32[128]{0:T(128)}, u32[]{:S(2)}) %copy-start.2) | copy-done | bytes 536
  2.6 0.0 copy-start
  2.6 0.9 %copy-done = bf16[128,1024]{1,0:T(8,128)(2,1)S(1)} copy-done((bf16[128,1024]{1,0:T(8,128)(2,1)S(1)}, bf16[128,1024]{1,0:T(8,128)(2,1)}, u32[]{:S(2)}) %copy-start) | copy-done | bytes 262168
  3.5 0.0 copy-start.1
  3.5 0.9 %copy-done.1 = bf16[128,1024]{1,0:T(8,128)(2,1)S(1)} copy-done((bf16[128,1024]{1,0:T(8,128)(2,1)S(1)}, bf16[128,1024]{1,0:T(8,128)(2,1)}, u32[]{:S(2)}) %copy-start.1) | copy-done | bytes 262168
  4.5 47.5 %shard_map.92 = (f32[1,128]{1,0:T(1,128)S(1)}, f32[128,1024]{1,0:T(8,128)S(1)}, f32[128,1024]{1,0:T(8,128)S(1)}, f32[1]{0:T(128)}, f32[1]{0:T(128)}) custom-call(bf16[128,1024]{1,0:T(8,128)(2,1)S(1)} %copy-done, bf16[8,16,1024]{2,1,0:T(8,128)(2,1)S(1)} %bitcast.9, s32[1,128]{1,0:T(1,128)S(1)} %bitcast.10, f32[1]{0:T(128)} %bitcast.7.temp_ref, f32[1]{0:T(128)} %bitcast.8.bias_ref), custom_call_target="tpu_custom_call" | custom-call | tf_op jit(solution)/shard_map/pallas_call | solution.py:340
  52.0 0.5 copy.17
  52.5 0.8 %copy.18 = f32[128,1024]{1,0:T(8,128)} copy(f32[128,1024]{1,0:T(8,128)S(1)} %get-tuple-element.21) | data formatting | bytes 1048576
  53.3 0.8 %copy.19 = f32[128,1024]{1,0:T(8,128)} copy(f32[128,1024]{1,0:T(8,128)S(1)} %get-tuple-element.22) | data formatting | bytes 1048576
Async XLA Ops:
  1.9 0.7 %copy-start.2 = (s32[128]{0:T(128)S(1)}, s32[128]{0:T(128)}, u32[]{:S(2)}) copy-start(s32[128]{0:T(128)} %param.7) | copy-start | bytes 1540
  2.6 0.9 %copy-start = (bf16[128,1024]{1,0:T(8,128)(2,1)S(1)}, bf16[128,1024]{1,0:T(8,128)(2,1)}, u32[]{:S(2)}) copy-start(bf16[128,1024]{1,0:T(8,128)(2,1)} %x_ref.1) | copy-start | bytes 786436
  3.5 0.9 %copy-start.1 = (bf16[128,1024]{1,0:T(8,128)(2,1)S(1)}, bf16[128,1024]{1,0:T(8,128)(2,1)}, u32[]{:S(2)}) copy-start(bf16[128,1024]{1,0:T(8,128)(2,1)} %param.6) | copy-start | bytes 786436
